TPU v7x, 256 devices: a whole 4x4x8 slice. The times are simulated.
256 devices in a mesh: space: 32 (over y, z), dp: 8 (over x, core).
Axes of the slice: x: 4, y: 4, z: 8, core: 2. Of those that a mesh axis runs over, the one named last changes fastest.
Arguments:
- tokens: bfloat16 [8, 256, 32, 512], P('dp', 'space'), may hold values from -6 to 6
- region: int32 [8, 64, 8], P('dp'), may hold values from 0 to 2
- valid: int32 [8, 256, 32], P('dp'), may hold values 0 or 1
- qkv_weight: bfloat16 [512, 1536], replicated, may hold values from -0.25 to 0.25
- proj_weight: bfloat16 [512, 512], replicated, may hold values from -0.25 to 0.25
- merge_weight: bfloat16 [2048, 1024], replicated, may hold values from -0.125 to 0.125
- logit_scale: float32 [16], replicated, may hold values from 4 to 100
- bias_table: float32 [16, 225], replicated, may hold values from -8 to 8
- gain_attn: float32 [512], replicated, may hold values from 0.5 to 1.5
- gain_merge: float32 [1024], replicated, may hold values from 0.5 to 1.5
- cotangent: bfloat16 [8, 128, 16, 1024], P('dp', 'space'), may hold values from -6 to 6
Outputs:
- merged: bfloat16 [8, 128, 16, 1024], P('dp', 'space')
- grad_tokens: bfloat16 [8, 256, 32, 512], P('dp', 'space')
- grad_qkv: float32 [512, 1536], P('space', 'dp')
- grad_proj: float32 [512, 512], P('space', 'dp')
- grad_merge: float32 [2048, 1024], P('space', 'dp')
- grad_bias: float32 [16, 225], replicated
All inputs are finite; a program needn't handle non-finite values. No bound on the sum of `valid` on one device may be relied on, other than what follows from the above.
Results may differ from a plain program's by a relative error of at most 0.038.
Values may be sent and summed in bfloat16 or wider, within the bound.
A program may use at most 128 MiB of HBM per device.

v0:
```python
import jax
import jax.numpy as jnp
import numpy as np
from jax import lax
from jax.experimental import pallas as pl
from jax.experimental.pallas import tpu as pltpu
from jax.sharding import PartitionSpec as P

WIN = 8
HEAD_DIM = 32
SHIFT = 4
OFFSETS = 225
NX, NY, NZ, CORES = 4, 4, 8, 2
LANES = 128
MESH = pl.DeviceIdType.MESH


class Place:
    def __init__(self):
        strip, image = lax.axis_index("space"), lax.axis_index("dp")
        self.y, self.z = strip // NZ, lax.rem(strip, NZ)
        self.x, self.c = image // CORES, lax.rem(image, CORES)

    def at(self, x=None, y=None, z=None, c=None):
        x = self.x if x is None else x
        y = self.y if y is None else y
        z = self.z if z is None else z
        c = self.c if c is None else c
        return (y * NZ + z, x * CORES + c)

    def along(self, axis, step):
        count = {"x": NX, "y": NY, "z": NZ, "c": CORES}[axis]
        return self.at(**{axis: lax.rem(getattr(self, axis) + step, count)})

    def partners(self):
        return (
            [self.along("c", 1)]
            + [self.along("x", step) for step in range(1, NX)]
            + [self.along("y", step) for step in range(1, NY)]
            + [self.along("z", step) for step in range(1, NZ)]
        )


class Sems:
    def __init__(self, send, recv):
        self.send, self.recv, self.used = send, recv, 0

    def copy(self, source, target, device):
        index = self.used
        self.used += 1
        made = pltpu.make_async_remote_copy(
            src_ref=source,
            dst_ref=target,
            send_sem=self.send.at[index],
            recv_sem=self.recv.at[index],
            device_id=device,
            device_id_type=MESH,
        )
        made.start()
        return made


def add_blocks(count, put, parts):
    def body(index, carry):
        total = parts[0](index).astype(jnp.float32)
        for part in parts[1:]:
            total = total + part(index).astype(jnp.float32)
        put(index, total.astype(jnp.bfloat16))
        return carry

    lax.fori_loop(0, count, body, 0)


def ring_sum(place, sems, axis, held, halves, blocks, far_lo, far_hi, from_dn, from_up, out):
    me = getattr(place, axis)
    up, dn, far = lax.rem(me + 1, 4), lax.rem(me + 3, 4), lax.rem(me + 2, 4)
    to_up, to_dn = place.along(axis, 1), place.along(axis, 3)
    half = blocks // 2
    lo, hi = pl.ds(0, half), pl.ds(half, half)
    one = sems.copy(held.at[far, lo], far_lo, to_up)
    two = sems.copy(held.at[far, hi], far_hi, to_dn)
    three = sems.copy(held.at[up, hi], from_dn.at[hi], to_up)
    four = sems.copy(held.at[dn, lo], from_up.at[lo], to_dn)
    yield

    def put_up(i, v):
        held[up, i] = v

    def put_dn(i, v):
        held[dn, half + i] = v

    one.wait_recv()
    add_blocks(half, put_up, [lambda i: held[up, i], lambda i: far_lo[i]])
    five = sems.copy(held.at[up, lo], from_dn.at[lo], to_up)
    yield
    two.wait_recv()
    add_blocks(half, put_dn, [lambda i: held[dn, half + i], lambda i: far_hi[i]])
    six = sems.copy(held.at[dn, hi], from_up.at[hi], to_dn)
    yield
    three.wait_recv()
    four.wait_recv()
    five.wait_recv()
    six.wait_recv()

    def put_out(i, v):
        out[i] = v

    add_blocks(
        blocks, put_out, [lambda i: held[me, i], lambda i: from_dn[i], lambda i: from_up[i]]
    )
    for copy in (one, two, three, four, five, six):
        copy.wait_send()


def stream_scratch(rows):
    full = NZ * rows
    shapes = [
        (4, 4, full, LANES),
        (4, 4, full, LANES),
        (2, full, LANES),
        (2, full, LANES),
        (4, full, LANES),
        (4, full, LANES),
        (4, NZ, rows, LANES),
        (NZ // 2, rows, LANES),
        (NZ // 2, rows, LANES),
        (NZ, rows, LANES),
        (NZ, rows, LANES),
        (NZ, rows, LANES),
        (NZ, rows, LANES),
    ]
    return [pltpu.VMEM(shape, jnp.bfloat16) for shape in shapes]


STREAM_COPIES = 1 + 6 + 6 + (NZ - 1)


def stream(place, sems, first, second, rows, source, out, bufs):
    other, core, a1, a2, a3, a4, one, b1, b2, b3, b4, two, last = bufs
    mine = place.c
    cross = sems.copy(source.at[1 - mine], other, place.along("c", 1))
    yield
    cross.wait_recv()

    def put_core(i, v):
        core[i // 4, lax.rem(i, 4)] = v

    add_blocks(
        16,
        put_core,
        [
            lambda i: source[mine, i // 4, lax.rem(i, 4)],
            lambda i: other[i // 4, lax.rem(i, 4)],
        ],
    )

    class Fold:
        def __setitem__(self, i, v):
            one[i] = v.reshape(NZ, rows, LANES)

    yield from ring_sum(place, sems, first, core, None, 4, a1, a2, a3, a4, Fold())
    yield from ring_sum(place, sems, second, one, None, NZ, b1, b2, b3, b4, two)
    sent = []
    for step in range(1, NZ):
        target = lax.rem(place.z + step, NZ)
        sent.append(sems.copy(two.at[target], last.at[step], place.along("z", step)))
    yield
    total = two[place.z].astype(jnp.float32)
    for step in range(1, NZ):
        sent[step - 1].wait_recv()
        total = total + last[step].astype(jnp.float32)
    out[...] = total
    for copy in sent:
        copy.wait_send()
    cross.wait_send()


BIAS_ROWS, BIAS_LANES = 16, 256
BIAS_COPIES = 1 + (NX - 1) + (NY - 1) + (NZ - 1)


def bias_scratch():
    return [
        pltpu.VMEM((count, BIAS_ROWS, BIAS_LANES), jnp.float32)
        for count in (CORES, NX, NY, NZ)
    ]


def bias_sum(place, sems, value, out, bufs):
    copies = []
    for axis, count, buf in zip("cxyz", (CORES, NX, NY, NZ), bufs):
        me = getattr(place, axis)
        buf[me] = value
        sent = [
            sems.copy(buf.at[me], buf.at[me], place.along(axis, step)) for step in range(1, count)
        ]
        yield
        for copy in sent:
            copy.wait_recv()
        value = buf[0]
        for index in range(1, count):
            value = value + buf[index]
        copies += sent
    out[...] = value
    for copy in copies:
        copy.wait_send()


def run_all(tasks):
    tasks = list(tasks)
    while tasks:
        for task in list(tasks):
            try:
                next(task)
            except StopIteration:
                tasks.remove(task)


def enter(partners):
    barrier = pltpu.get_barrier_semaphore()
    for device in partners:
        pl.semaphore_signal(barrier, inc=1, device_id=device, device_id_type=MESH)
    pl.semaphore_wait(barrier, len(partners))


F32, BF16 = jnp.float32, jnp.bfloat16
TOKENS, D, GROUPS = 256, 512, 4
HALF = TOKENS // 2
PLACES = WIN * WIN
WIDE = 4 * PLACES


def nn(a, b):
    return lax.dot_general(a, b, (((1,), (0,)), ((), ())), preferred_element_type=F32)


def nt(a, b):
    return lax.dot_general(a, b, (((1,), (1,)), ((), ())), preferred_element_type=F32)


def tn(a, b):
    return lax.dot_general(a, b, (((0,), (0,)), ((), ())), preferred_element_type=F32)


def split2(t):
    high = t.astype(BF16)
    return high, (t - high.astype(F32)).astype(BF16)


def split3(t):
    high = t.astype(BF16)
    rest = t - high.astype(F32)
    middle = rest.astype(BF16)
    return high, middle, (rest - middle.astype(F32)).astype(BF16)


def iota(shape, axis):
    return lax.broadcasted_iota(jnp.int32, shape, axis)


def constants():
    half, w, r, c = np.meshgrid(*[np.arange(n) for n in (2, 4, 4, 8)], indexing="ij")
    natural = (half * 4 + r) * 32 + (w * 8 + c + SHIFT) % 32
    strip = np.eye(TOKENS, dtype=np.float32)[natural.reshape(-1)]
    k, rp, b = np.meshgrid(np.arange(4), np.arange(2), np.arange(16), indexing="ij")
    column = (2 * b + k // 2 - SHIFT) % 32
    place = (column // 8) * 32 + (2 * rp + k % 2) * 8 + column % 8
    quad = np.eye(HALF, dtype=np.float32)[place.reshape(-1)]
    ct, lane = np.meshgrid(np.arange(8), np.arange(128), indexing="ij")
    offset = np.where(lane < 120, (lane // 8) * 15 + lane % 8 - ct + 7, -1)
    onehot = (np.arange(256)[:, None] == offset.reshape(1, -1)).astype(np.float32)
    lanes = np.arange(256) % 128 // HEAD_DIM
    heads = (lanes[:, None] == lanes[None, :128]).astype(np.float32)
    return [jnp.asarray(t, BF16) for t in (strip, quad, onehot, heads)]


def head_sum(t, heads):
    return nn(jnp.concatenate(split2(t), axis=1), heads)


def stack_heads(t, lane_masks):
    return jnp.concatenate([t * mask for mask in lane_masks], axis=0)


def fold_heads(t, lane_masks):
    total = t[:PLACES] * lane_masks[0]
    for h in range(1, 4):
        total = total + t[h * PLACES : (h + 1) * PLACES] * lane_masks[h]
    return total


def norm_parts(t):
    centred = t - jnp.mean(t, -1, keepdims=True)
    scale = lax.rsqrt(jnp.mean(centred * centred, -1, keepdims=True) + 1e-05)
    return centred * scale, scale


def norm_back(grad, hat, scale):
    return scale * (
        grad - jnp.mean(grad, -1, keepdims=True) - hat * jnp.mean(grad * hat, -1, keepdims=True)
    )


def window_masks(place, region_ref, valid_ref, mask_ref):
    strip = place.y * NZ + place.z
    place_lane = iota((1, WIDE), 1) % PLACES
    row, col = place_lane // WIN, place_lane % WIN
    region = region_ref[...].astype(F32)
    valid = valid_ref[...].astype(F32)
    source_row = lax.rem(strip * WIN + SHIFT + row, 256)
    region_row = iota((64, WIDE), 0) == source_row // 4
    valid_row = iota((256, WIDE), 0) == source_row
    shifted_row = strip * WIN + row
    row_part = jnp.where(shifted_row < 256 - WIN, 0, jnp.where(shifted_row < 256 - SHIFT, 1, 2))
    diagonal = iota((PLACES, WIDE), 0) == place_lane
    pick = (iota((PLACES, WIDE), 0) == iota((PLACES, WIDE), 1)).astype(F32)
    for w in range(4):
        source_col = lax.rem(w * WIN + SHIFT + col, 32)
        shifted_col = w * WIN + col
        col_part = jnp.where(shifted_col < 32 - WIN, 0, jnp.where(shifted_col < 32 - SHIFT, 1, 2))
        region_pick = (iota((8, WIDE), 0) == source_col // 4).astype(F32)
        valid_pick = (iota((32, WIDE), 0) == source_col).astype(F32)
        swath = jnp.sum(jnp.where(region_row, nn(region, region_pick), 0.0), 0, keepdims=True)
        live = jnp.sum(jnp.where(valid_row, nn(valid, valid_pick), 0.0), 0, keepdims=True)
        label = swath * 9.0 + (row_part * 3 + col_part).astype(F32)
        label_key = jnp.sum(pick * label, 1, keepdims=True)
        live_key = jnp.sum(pick * live, 1, keepdims=True)
        same = (label_key == label).astype(F32)
        open_key = jnp.where(diagonal, 1.0, jnp.where(live_key == 1.0, 1.0, 0.0))
        mask_ref[w] = same * open_key


def spread_bias(table_ref, onehot_ref, padded_ref, grid_ref, bias_ref):
    padded_ref[...] = jnp.zeros_like(padded_ref)
    padded_ref[:, :OFFSETS] = table_ref[...]
    parts = nn(jnp.concatenate(split3(padded_ref[...]), axis=0), onehot_ref[...])
    spread = parts[:16] + parts[16:32] + parts[32:]
    for ct in range(8):
        grid_ref[pl.ds(ct, 16, stride=8), :] = spread[:, ct * 128 : (ct + 1) * 128]
    left = iota((8, 128), 1) < PLACES
    for pair in range(8):
        even = grid_ref[pair * 16 : pair * 16 + 8]
        odd = grid_ref[pair * 16 + 8 : pair * 16 + 16]
        lanes = pl.ds(pair % 2 * 128, 128)
        for rt in range(8):
            shift = (7 - rt) * 8
            bias_ref[pair // 2, rt * 8 : rt * 8 + 8, lanes] = jnp.where(
                left,
                pltpu.roll(even, (128 - shift) % 128, 1),
                pltpu.roll(odd, (128 + 64 - shift) % 128, 1),
            )


def gather_bias(acc_ref, onehot_ref, grid_ref):
    left = iota((8, 128), 1) < PLACES
    for pair in range(8):
        lanes = pl.ds(pair % 2 * 128, 128)
        even = jnp.zeros((8, 128), F32)
        odd = jnp.zeros((8, 128), F32)
        for rt in range(8):
            shift = (7 - rt) * 8
            piece = acc_ref[pair // 2, rt * 8 : rt * 8 + 8, lanes]
            even = even + pltpu.roll(jnp.where(left, piece, 0.0), shift, 1)
            odd = odd + pltpu.roll(jnp.where(left, 0.0, piece), (64 + shift) % 128, 1)
        grid_ref[pair * 16 : pair * 16 + 8] = even
        grid_ref[pair * 16 + 8 : pair * 16 + 16] = odd
    grid = jnp.concatenate([grid_ref[pl.ds(ct, 16, stride=8), :] for ct in range(8)], axis=1)
    parts = nt(jnp.concatenate(split3(grid), axis=0), onehot_ref[...])
    return parts[:16] + parts[16:32] + parts[32:]


def window_rows(w):
    return (
        pl.ds(pl.multiple_of(w * 32, 32), 32),
        pl.ds(pl.multiple_of(HALF + w * 32, 32), 32),
    )


def take(ref, w, start):
    first, second = window_rows(w)
    lanes = slice(start, start + LANES)
    return jnp.concatenate([ref[first, lanes], ref[second, lanes]], axis=0)


def put(ref, w, start, value):
    first, second = window_rows(w)
    lanes = slice(start, start + LANES)
    ref[first, lanes] = value[:32]
    ref[second, lanes] = value[32:]


def block_kernel(
    tok_ref,
    region_ref,
    valid_ref,
    wq_ref,
    wp_ref,
    wm_hbm,
    scale_ref,
    table_ref,
    gain_attn_ref,
    gain_merge_ref,
    cot_ref,
    strip_ref,
    quad_ref,
    onehot_ref,
    heads_ref,
    merged_out,
    tokens_out,
    qkv_out,
    proj_out,
    merge_out,
    bias_out,
    wm_ref,
    tw_ref,
    x_ref,
    qkv_ref,
    inv_ref,
    qh_ref,
    ql_ref,
    kh_ref,
    kl_ref,
    mask_ref,
    padded_ref,
    grid_ref,
    bias_ref,
    probs_ref,
    mixed_ref,
    normed_ref,
    hat_ref,
    normed_in,
    quads_ref,
    gh_ref,
    gn_ref,
    go_ref,
    roll_ref,
    gm_ref,
    dn_ref,
    act_ref,
    gs_ref,
    gs_in,
    acc_ref,
    sum_a,
    sum_b,
    part_a,
    part_b,
    sum_c,
    sum_d,
    *scratch,
):
    many = len(stream_scratch(32))
    bufs = [scratch[i * many : (i + 1) * many] for i in range(4)]
    bias_bufs = scratch[4 * many : 4 * many + 4]
    send, recv, local = scratch[4 * many + 4 :]
    place = Place()
    sems = Sems(send, recv)
    load = pltpu.make_async_copy(wm_hbm, wm_ref, local)
    load.start()

    strip = place.y * NZ + place.z
    image = place.x * CORES + place.c
    after = (lax.rem(strip + 1, NY * NZ), image)
    before = (lax.rem(strip + NY * NZ - 1, NY * NZ), image)
    own, far = slice(0, HALF), slice(HALF, TOKENS)

    tw_ref[...] = nn(strip_ref[...], tok_ref[...]).astype(BF16)
    enter(place.partners() + [after, before])
    halo_tokens = sems.copy(tw_ref.at[own], x_ref.at[far], before)
    x_ref[own] = tw_ref[far]

    lane = iota((1, LANES), 1)
    masks = [(lane // HEAD_DIM == h).astype(F32) for h in range(4)]
    masks16 = [mask.astype(BF16) for mask in masks]
    scales = []
    for g in range(GROUPS):
        row = jnp.zeros((1, LANES), F32)
        for h in range(4):
            row = row + masks[h] * scale_ref[g * 4 + h]
        scales.append(row)
    heads = heads_ref[...]

    qkv_ref[own] = nn(x_ref[own], wq_ref[...]).astype(BF16)
    window_masks(place, region_ref, valid_ref, mask_ref)
    spread_bias(table_ref, onehot_ref, padded_ref, grid_ref, bias_ref)
    halo_tokens.wait_recv()
    qkv_ref[far] = nn(x_ref[far], wq_ref[...]).astype(BF16)

    for g in range(GROUPS):
        cols = slice(g * LANES, (g + 1) * LANES)
        for part, high, low in ((0, qh_ref, ql_ref), (D, kh_ref, kl_ref)):
            raw = qkv_ref[:, part + g * LANES : part + (g + 1) * LANES].astype(F32)
            inverse = lax.rsqrt(head_sum(raw * raw, heads) + 1e-06)
            inv_ref[:, part + g * LANES : part + (g + 1) * LANES] = inverse
            unit = raw * inverse
            if part == 0:
                unit = unit * scales[g]
            a, b = split2(unit)
            high[:, cols] = a
            low[:, cols] = b

    def forward(w, carry):
        allowed = mask_ref[w] > 0.5
        for g in range(GROUPS):
            start = g * LANES
            kh, kl = take(kh_ref, w, start), take(kl_ref, w, start)
            qh = stack_heads(take(qh_ref, w, start), masks16)
            ql = stack_heads(take(ql_ref, w, start), masks16)
            score = nt(
                jnp.concatenate([kh, kl, kh], axis=1), jnp.concatenate([qh, qh, ql], axis=1)
            )
            score = jnp.where(allowed, score + bias_ref[g], -1000000000.0)
            expo = jnp.exp(score - jnp.max(score, 0, keepdims=True))
            probs = expo * (1.0 / jnp.sum(expo, 0, keepdims=True))
            probs_ref[w, g] = probs
            out = tn(probs.astype(BF16), take(qkv_ref, w, 2 * D + start))
            put(mixed_ref, w, start, fold_heads(out, masks).astype(BF16))
        return carry

    lax.fori_loop(0, 4, forward, 0)

    gain_attn = gain_attn_ref[...]

    def project(rows):
        hat, scale = norm_parts(nn(mixed_ref[rows], wp_ref[...]))
        hat_ref[rows] = hat
        normed_ref[rows] = (hat * gain_attn).astype(BF16)
        return scale

    scale_far = project(far)
    halo_normed = sems.copy(normed_ref.at[far], normed_in, after)
    scale_own = project(own)

    def make_quads(which, added):
        rows = slice(which * HALF, (which + 1) * HALF)
        hidden = (tw_ref[rows].astype(F32) + added.astype(F32)).astype(BF16)
        sorted_rows = nn(quad_ref[...], hidden).astype(BF16)
        for k in range(4):
            quads_ref[which * 32 : which * 32 + 32, k * D : (k + 1) * D] = sorted_rows[
                k * 32 : (k + 1) * 32
            ]

    make_quads(1, normed_ref[own])
    load.wait()
    halo_normed.wait_recv()
    make_quads(0, normed_in[...])

    gain_merge = gain_merge_ref[...]
    hat, scale = norm_parts(nn(quads_ref[...], wm_ref[...]))
    merged_out[...] = (hat * gain_merge).astype(BF16)
    grad_pre = norm_back(cot_ref[...].astype(F32) * gain_merge, hat, scale).astype(BF16)
    grad_quads = nt(grad_pre, wm_ref[...]).astype(BF16)
    for which in range(2):
        stacked = jnp.concatenate(
            [grad_quads[which * 32 : which * 32 + 32, k * D : (k + 1) * D] for k in range(4)],
            axis=0,
        )
        gh_ref[which * HALF : (which + 1) * HALF] = tn(quad_ref[...], stacked).astype(BF16)
        if which == 0:
            halo_hidden = sems.copy(gh_ref.at[own], gn_ref.at[far], before)
    gn_ref[own] = gh_ref[far]

    for x in range(NX):
        for y in range(NY):
            block = tn(
                quads_ref[:, y * D : (y + 1) * D], grad_pre[:, x * 256 : (x + 1) * 256]
            ).reshape(NZ, 2, 32, 256)
            for c in range(CORES):
                lanes = slice(c * LANES, (c + 1) * LANES)
                sum_a[c, x, y] = block[:, 0, :, lanes].reshape(NZ * 32, LANES).astype(BF16)
                sum_b[c, y, x] = block[:, 1, :, lanes].reshape(NZ * 32, LANES).astype(BF16)

    tasks = [
        stream(place, sems, "x", "y", 32, sum_a, merge_out.at[0:32], bufs[0]),
        stream(place, sems, "y", "x", 32, sum_b, merge_out.at[32:64], bufs[1]),
    ]

    def pump():
        for task in list(tasks):
            try:
                next(task)
            except StopIteration:
                tasks.remove(task)

    pump()

    def back_norm(rows, scale):
        grad = gn_ref[rows].astype(F32) * gain_attn
        out = norm_back(grad, hat_ref[rows], scale)
        go_ref[rows] = out.astype(BF16)
        for x in range(NX):
            lanes = slice(x * LANES, (x + 1) * LANES)
            roll_ref[rows, lanes] = pltpu.roll(out[:, lanes], 64, 1).astype(BF16)
        gm_ref[rows] = nt(go_ref[rows], wp_ref[...]).astype(BF16)

    back_norm(own, scale_own)
    halo_hidden.wait_recv()
    back_norm(far, scale_far)
    pump()

    acc_ref[...] = jnp.zeros_like(acc_ref)

    def backward(w, carry):
        for g in range(GROUPS):
            start = g * LANES
            grad = stack_heads(take(gm_ref, w, start), masks16)
            probs = probs_ref[w, g]
            grad_probs = nt(take(qkv_ref, w, 2 * D + start), grad)
            put(act_ref, w, 2 * D + start, nn(probs.astype(BF16), grad).astype(BF16))
            weighted = probs * grad_probs
            grad_score = weighted - probs * jnp.sum(weighted, 0, keepdims=True)
            acc_ref[g] += grad_score
            grad_score = grad_score.astype(BF16)
            query = stack_heads(take(qh_ref, w, start), masks16)
            put(dn_ref, w, D + start, nn(grad_score, query))
            put(dn_ref, w, start, fold_heads(tn(grad_score, take(kh_ref, w, start)), masks))
        return carry

    lax.fori_loop(0, 2, backward, 0)
    pump()
    lax.fori_loop(2, 4, backward, 0)
    pump()

    for g in range(GROUPS):
        for part in (0, D):
            cols = slice(part + g * LANES, part + (g + 1) * LANES)
            grad = dn_ref[:, cols]
            if part == 0:
                grad = grad * scales[g]
            inverse = inv_ref[:, cols]
            unit = qkv_ref[:, cols].astype(F32) * inverse
            act_ref[:, cols] = (inverse * (grad - unit * head_sum(unit * grad, heads))).astype(BF16)

    gs_ref[far] = nt(act_ref[far], wq_ref[...]).astype(BF16)
    halo_shifted = sems.copy(gs_ref.at[far], gs_in, after)
    pump()

    bias_part = gather_bias(acc_ref, onehot_ref, grid_ref)
    left = iota((1, LANES), 1) < 64
    for x in range(NX):
        block = tn(x_ref[...], act_ref[:, x * 384 : (x + 1) * 384])
        rolled = tn(mixed_ref[...], roll_ref[:, x * LANES : (x + 1) * LANES])
        middle = block[:, 128:256]
        firsts = (block[:, :128], block[:, 256:])
        seconds = (jnp.where(left, middle, rolled), jnp.where(left, rolled, middle))
        for c in range(CORES):
            one, two = firsts[c].astype(BF16), seconds[c].astype(BF16)
            for y in range(NY):
                rows = slice(y * 128, (y + 1) * 128)
                sum_c[c, x, y] = one[rows]
                sum_d[c, y, x] = two[rows]
    tasks += [
        stream(place, sems, "x", "y", 16, sum_c, part_a, bufs[2]),
        stream(place, sems, "y", "x", 16, sum_d, part_b, bufs[3]),
        bias_sum(place, sems, bias_part, padded_ref, bias_bufs),
    ]
    pump()

    gs_ref[own] = nt(act_ref[own], wq_ref[...]).astype(BF16)
    gs_ref[own] = (gh_ref[far].astype(F32) + gs_ref[own].astype(F32)).astype(BF16)
    halo_shifted.wait_recv()
    gn_own = (gh_ref[own].astype(F32) + gs_in[...].astype(F32)).astype(BF16)
    tokens_out[...] = tn(strip_ref[...], jnp.concatenate([gn_own, gs_ref[own]], axis=0)).astype(
        BF16
    )
    run_all(tasks)
    for copy in (halo_tokens, halo_normed, halo_hidden, halo_shifted):
        copy.wait_send()

    bias_out[...] = padded_ref[:, :OFFSETS]
    one, two = part_a[...], part_b[...]
    one_rolled, two_rolled = pltpu.roll(one, 64, 1), pltpu.roll(two, 64, 1)
    first_core = place.c == 0
    qkv_out[:, :128] = jnp.where(first_core, one, jnp.where(left, two_rolled, one_rolled))
    qkv_out[:, 128:] = jnp.where(first_core, two, one_rolled)[:, :64]
    proj_out[...] = jnp.where(first_core, two_rolled, two)[:, :64]


def block(tokens, region, valid, wq, wp, wm, scale, table, gain_attn, gain_merge, cot):
    vmem = pl.BlockSpec(memory_space=pltpu.VMEM)
    smem = pl.BlockSpec(memory_space=pltpu.SMEM)
    total = 4 + 4 * STREAM_COPIES + BIAS_COPIES

    def buf(*shape):
        return pltpu.VMEM(shape, BF16)

    def wide(*shape):
        return pltpu.VMEM(shape, F32)

    return pl.pallas_call(
        block_kernel,
        out_shape=[
            jax.ShapeDtypeStruct((64, 1024), BF16),
            jax.ShapeDtypeStruct((TOKENS, D), BF16),
            jax.ShapeDtypeStruct((16, 192), F32),
            jax.ShapeDtypeStruct((16, 64), F32),
            jax.ShapeDtypeStruct((64, 128), F32),
            jax.ShapeDtypeStruct((16, OFFSETS), F32),
        ],
        in_specs=[vmem] * 5 + [pl.BlockSpec(memory_space=pl.ANY), smem] + [vmem] * 8,
        out_specs=[vmem] * 6,
        scratch_shapes=[
            buf(2048, 1024),
            buf(TOKENS, D),
            buf(TOKENS, D),
            buf(TOKENS, 3 * D),
            wide(TOKENS, 2 * D),
            buf(TOKENS, D),
            buf(TOKENS, D),
            buf(TOKENS, D),
            buf(TOKENS, D),
            wide(4, PLACES, WIDE),
            wide(BIAS_ROWS, BIAS_LANES),
            wide(128, 128),
            wide(GROUPS, PLACES, WIDE),
            wide(4, GROUPS, PLACES, WIDE),
            buf(TOKENS, D),
            buf(TOKENS, D),
            wide(TOKENS, D),
            buf(HALF, D),
            buf(64, 2048),
            buf(TOKENS, D),
            buf(TOKENS, D),
            buf(TOKENS, D),
            buf(TOKENS, D),
            buf(TOKENS, D),
            wide(TOKENS, 2 * D),
            buf(TOKENS, 3 * D),
            buf(TOKENS, D),
            buf(HALF, D),
            wide(GROUPS, PLACES, WIDE),
            buf(CORES, NX, NY, NZ * 32, LANES),
            buf(CORES, NY, NX, NZ * 32, LANES),
            wide(16, LANES),
            wide(16, LANES),
            buf(CORES, NX, NY, NZ * 16, LANES),
            buf(CORES, NY, NX, NZ * 16, LANES),
        ]
        + stream_scratch(32)
        + stream_scratch(32)
        + stream_scratch(16)
        + stream_scratch(16)
        + bias_scratch()
        + [
            pltpu.SemaphoreType.DMA((total,)),
            pltpu.SemaphoreType.DMA((total,)),
            pltpu.SemaphoreType.DMA,
        ],
        compiler_params=pltpu.CompilerParams(
            collective_id=0, has_side_effects=True, vmem_limit_bytes=56 * 1024 * 1024
        ),
        name="block",
    )(tokens, region, valid, wq, wp, wm, scale, table, gain_attn, gain_merge, cot, *constants())


def shards(
    tokens,
    region,
    valid,
    qkv_weight,
    proj_weight,
    merge_weight,
    logit_scale,
    bias_table,
    gain_attn,
    gain_merge,
    cotangent,
):
    merged, grad_tokens, grad_qkv, grad_proj, grad_merge, grad_bias = block(
        tokens.reshape(TOKENS, D),
        region[0],
        valid[0],
        qkv_weight,
        proj_weight,
        merge_weight,
        logit_scale,
        bias_table,
        gain_attn[None],
        gain_merge[None],
        cotangent.reshape(64, 1024),
    )
    return (
        merged.reshape(cotangent.shape),
        grad_tokens.reshape(tokens.shape),
        grad_qkv,
        grad_proj,
        grad_merge,
        grad_bias,
    )


def solution(mesh):
    return jax.shard_map(
        shards,
        mesh=mesh,
        in_specs=(
            P("dp", "space", None, None),
            P("dp", None, None),
            P("dp", None, None),
            P(),
            P(),
            P(),
            P(),
            P(),
            P(),
            P(),
            P("dp", "space", None, None),
        ),
        out_specs=(
            P("dp", "space", None, None),
            P("dp", "space", None, None),
            P("space", "dp"),
            P("space", "dp"),
            P("space", "dp"),
            P(),
        ),
        check_vma=False,
    )
```

profile of v0, /device:TPU:32, one launch (start us, length us, event | category | flops | bytes accessed | tf_op | source)
XLA Modules:
  0.0 91.5 jit_solution(11470887062845552282)
XLA Ops:
  0.6 1.4 %copy.21 = s32[1,64,8]{2,1,0:T(8,128)} copy(s32[1,64,8]{1,2,0:T(8,128)} %param.16) | data formatting | bytes 4096 | tf_op args[1]
  2.0 1.5 %copy.22 = s32[1,256,32]{2,1,0:T(8,128)} copy(s32[1,256,32]{1,2,0:T(8,128)} %param.17) | data formatting | bytes 65536 | tf_op args[2]
  3.5 79.4 %block.1 = (bf16[64,1024]{1,0:T(8,128)(2,1)}, bf16[256,512]{1,0:T(8,128)(2,1)}, f32[16,192]{1,0:T(8,128)}, f32[16,64]{1,0:T(8,128)}, f32[64,128]{1,0:T(8,128)}, /*index=5*/f32[16,225]{1,0:T(8,128)}) custom-call(bf16[256,512]{1,0:T(8,128)(2,1)} %bitcast.9, s32[64,8]{1,0:T(8,128)} %bitcast.12, s32[256,32]{1,0:T(8,128)} %bitcast.8, bf16[512,1536]{1,0:T(8,128)(2,1)} %wq_ref.1, ...), custom_call_target="tpu_custom_call" | custom-call | tf_op jit(solution)/shard_map/block/pallas_call | solution.py:689
  83.0 1.6 %copy.29 = bf16[1,4,16,1024]{3,2,1,0:T(8,128)(2,1)} copy(bf16[1,4,16,1024]{3,2,1,0:T(8,128)(2,1)} %bitcast.13) | data formatting | bytes 262144
  84.5 1.7 %copy.30 = bf16[1,8,32,512]{3,2,1,0:T(8,128)(2,1)} copy(bf16[1,8,32,512]{3,2,1,0:T(8,128)(2,1)} %bitcast.10) | data formatting | bytes 524288
  86.2 1.3 %copy.31 = f32[16,192]{1,0:T(8,128)} copy(f32[16,192]{1,0:T(8,128)} %get-tuple-element.26) | data formatting | bytes 24576
  87.5 1.3 %copy.32 = f32[16,64]{1,0:T(8,128)} copy(f32[16,64]{1,0:T(8,128)} %get-tuple-element.27) | data formatting | bytes 8192
  88.8 1.4 %copy.33 = f32[64,128]{1,0:T(8,128)} copy(f32[64,128]{1,0:T(8,128)} %get-tuple-element.28) | data formatting | bytes 65536
  90.2 1.3 %copy.34 = f32[16,225]{1,0:T(8,128)} copy(f32[16,225]{1,0:T(8,128)} %get-tuple-element.29) | data formatting | bytes 28800
where the time goes:
time: 92.5 us; the launch traced here: 91.5 us
  Pallas kernels  79.4 us (86%)
  local copies, waits for them, and re-layouts  11.4 us (12%)
    pallas_call x1, Pallas kernels, block(): pl.pallas_call(block_kernel, out_shape=[jax.ShapeDtypeStruct((64, 1024),...  79.4 us
    unnamed x8, local copies, waits for them, and re-layouts  11.4 us

commit v1 on v0

--- a/solution.py
+++ b/solution.py
@@ -1,6 +1,7 @@
+import functools
+
 import jax
 import jax.numpy as jnp
-import numpy as np
 from jax import lax
 from jax.experimental import pallas as pl
 from jax.experimental.pallas import tpu as pltpu
@@ -68,10 +69,13 @@
         put(index, total.astype(jnp.bfloat16))
         return carry
 
-    lax.fori_loop(0, count, body, 0)
-
-
-def ring_sum(place, sems, axis, held, halves, blocks, far_lo, far_hi, from_dn, from_up, out):
+    if count == 1:
+        body(0, 0)
+    else:
+        lax.fori_loop(0, count, body, 0)
+
+
+def ring_sum(place, sems, axis, held, blocks, far_lo, far_hi, from_dn, from_up, put_out):
     me = getattr(place, axis)
     up, dn, far = lax.rem(me + 1, 4), lax.rem(me + 3, 4), lax.rem(me + 2, 4)
     to_up, to_dn = place.along(axis, 1), place.along(axis, 3)
@@ -101,10 +105,6 @@
     four.wait_recv()
     five.wait_recv()
     six.wait_recv()
-
-    def put_out(i, v):
-        out[i] = v
-
     add_blocks(
         blocks, put_out, [lambda i: held[me, i], lambda i: from_dn[i], lambda i: from_up[i]]
     )
@@ -112,31 +112,50 @@
         copy.wait_send()
 
 
-def stream_scratch(rows):
+def shot_sum(place, sems, axis, count, held, parts, blocks, arrived, out):
+    me = getattr(place, axis)
+    sent = []
+    for step in range(1, count):
+        target = lax.rem(me + step, count)
+        sent.append(
+            sems.copy(held.at[target], arrived.at[step - 1], place.along(axis, step))
+        )
+    yield
+    for copy in sent:
+        copy.wait_recv()
+    add_blocks(
+        blocks,
+        out,
+        [lambda i: parts(held, me, i)]
+        + [functools.partial(parts, arrived, step) for step in range(count - 1)],
+    )
+    for copy in sent:
+        copy.wait_send()
+
+
+def stream_scratch(rows, ring):
     full = NZ * rows
     shapes = [
         (4, 4, full, LANES),
         (4, 4, full, LANES),
-        (2, full, LANES),
-        (2, full, LANES),
-        (4, full, LANES),
-        (4, full, LANES),
         (4, NZ, rows, LANES),
-        (NZ // 2, rows, LANES),
-        (NZ // 2, rows, LANES),
+        (3, NZ, rows, LANES),
         (NZ, rows, LANES),
-        (NZ, rows, LANES),
-        (NZ, rows, LANES),
-        (NZ, rows, LANES),
+        (NZ - 1, rows, LANES),
     ]
+    if ring:
+        shapes += [(2, full, LANES), (2, full, LANES), (4, full, LANES), (4, full, LANES)]
+    else:
+        shapes += [(3, 4, full, LANES)]
     return [pltpu.VMEM(shape, jnp.bfloat16) for shape in shapes]
 
 
-STREAM_COPIES = 1 + 6 + 6 + (NZ - 1)
-
-
-def stream(place, sems, first, second, rows, source, out, bufs):
-    other, core, a1, a2, a3, a4, one, b1, b2, b3, b4, two, last = bufs
+def stream_copies(ring):
+    return 1 + (6 if ring else 3) + 3 + (NZ - 1)
+
+
+def stream(place, sems, first, second, rows, ring, source, out, bufs):
+    other, core, one, late, two, last = bufs[:6]
     mine = place.c
     cross = sems.copy(source.at[1 - mine], other, place.along("c", 1))
     yield
@@ -144,6 +163,12 @@
 
     def put_core(i, v):
         core[i // 4, lax.rem(i, 4)] = v
+
+    def put_one(i, v):
+        one[i] = v.reshape(NZ, rows, LANES)
+
+    def put_two(i, v):
+        two[...] = v
 
     add_blocks(
         16,
@@ -153,22 +178,24 @@
             lambda i: other[i // 4, lax.rem(i, 4)],
         ],
     )
-
-    class Fold:
-        def __setitem__(self, i, v):
-            one[i] = v.reshape(NZ, rows, LANES)
-
-    yield from ring_sum(place, sems, first, core, None, 4, a1, a2, a3, a4, Fold())
-    yield from ring_sum(place, sems, second, one, None, NZ, b1, b2, b3, b4, two)
+    if ring:
+        yield from ring_sum(place, sems, first, core, 4, *bufs[6:], put_one)
+    else:
+        yield from shot_sum(
+            place, sems, first, 4, core, lambda ref, k, i: ref[k, i], 4, bufs[6], put_one
+        )
+    yield from shot_sum(
+        place, sems, second, 4, one, lambda ref, k, i: ref[k], 1, late, put_two
+    )
     sent = []
     for step in range(1, NZ):
         target = lax.rem(place.z + step, NZ)
-        sent.append(sems.copy(two.at[target], last.at[step], place.along("z", step)))
+        sent.append(sems.copy(two.at[target], last.at[step - 1], place.along("z", step)))
     yield
     total = two[place.z].astype(jnp.float32)
     for step in range(1, NZ):
         sent[step - 1].wait_recv()
-        total = total + last[step].astype(jnp.float32)
+        total = total + last[step - 1].astype(jnp.float32)
     out[...] = total
     for copy in sent:
         copy.wait_send()
@@ -216,11 +243,14 @@
                 tasks.remove(task)
 
 
-def enter(partners):
+def greet(partners):
     barrier = pltpu.get_barrier_semaphore()
     for device in partners:
         pl.semaphore_signal(barrier, inc=1, device_id=device, device_id_type=MESH)
-    pl.semaphore_wait(barrier, len(partners))
+
+
+def enter(partners):
+    pl.semaphore_wait(pltpu.get_barrier_semaphore(), len(partners))
 
 
 F32, BF16 = jnp.float32, jnp.bfloat16
@@ -258,20 +288,38 @@
     return lax.broadcasted_iota(jnp.int32, shape, axis)
 
 
-def constants():
-    half, w, r, c = np.meshgrid(*[np.arange(n) for n in (2, 4, 4, 8)], indexing="ij")
-    natural = (half * 4 + r) * 32 + (w * 8 + c + SHIFT) % 32
-    strip = np.eye(TOKENS, dtype=np.float32)[natural.reshape(-1)]
-    k, rp, b = np.meshgrid(np.arange(4), np.arange(2), np.arange(16), indexing="ij")
-    column = (2 * b + k // 2 - SHIFT) % 32
-    place = (column // 8) * 32 + (2 * rp + k % 2) * 8 + column % 8
-    quad = np.eye(HALF, dtype=np.float32)[place.reshape(-1)]
-    ct, lane = np.meshgrid(np.arange(8), np.arange(128), indexing="ij")
-    offset = np.where(lane < 120, (lane // 8) * 15 + lane % 8 - ct + 7, -1)
-    onehot = (np.arange(256)[:, None] == offset.reshape(1, -1)).astype(np.float32)
-    lanes = np.arange(256) % 128 // HEAD_DIM
-    heads = (lanes[:, None] == lanes[None, :128]).astype(np.float32)
-    return [jnp.asarray(t, BF16) for t in (strip, quad, onehot, heads)]
+def bits(t, low, count):
+    return lax.bitwise_and(lax.shift_right_logical(t, low), (1 << count) - 1)
+
+
+def one_hot(match):
+    return jnp.where(match, 1.0, 0.0).astype(BF16)
+
+
+def strip_order():
+    i = iota((TOKENS, 1), 0)
+    column = lax.bitwise_and(bits(i, 5, 2) * 8 + bits(i, 0, 3) + SHIFT, 31)
+    natural = (bits(i, 7, 1) * 4 + bits(i, 3, 2)) * 32 + column
+    return one_hot(iota((TOKENS, TOKENS), 1) == natural)
+
+
+def quad_order():
+    i = iota((HALF, 1), 0)
+    column = lax.bitwise_and(2 * bits(i, 0, 4) + bits(i, 6, 1) + 32 - SHIFT, 31)
+    row = 2 * bits(i, 4, 1) + bits(i, 5, 1)
+    place = bits(column, 3, 2) * 32 + row * 8 + bits(column, 0, 3)
+    return one_hot(iota((HALF, HALF), 1) == place)
+
+
+def offset_order():
+    j = iota((1, 1024), 1)
+    offset = bits(j, 3, 4) * 15 + bits(j, 0, 3) - bits(j, 7, 3) + 7
+    offset = jnp.where(bits(j, 3, 4) < 15, offset, -1)
+    return one_hot(iota((256, 1024), 0) == offset)
+
+
+def head_order():
+    return one_hot(bits(iota((256, 128), 0), 5, 2) == bits(iota((256, 128), 1), 5, 2))
 
 
 def head_sum(t, heads):
@@ -320,8 +368,8 @@
         col_part = jnp.where(shifted_col < 32 - WIN, 0, jnp.where(shifted_col < 32 - SHIFT, 1, 2))
         region_pick = (iota((8, WIDE), 0) == source_col // 4).astype(F32)
         valid_pick = (iota((32, WIDE), 0) == source_col).astype(F32)
-        swath = jnp.sum(jnp.where(region_row, nn(region, region_pick), 0.0), 0, keepdims=True)
-        live = jnp.sum(jnp.where(valid_row, nn(valid, valid_pick), 0.0), 0, keepdims=True)
+        swath = jnp.sum(jnp.where(region_row, tn(region, region_pick), 0.0), 0, keepdims=True)
+        live = jnp.sum(jnp.where(valid_row, tn(valid, valid_pick), 0.0), 0, keepdims=True)
         label = swath * 9.0 + (row_part * 3 + col_part).astype(F32)
         label_key = jnp.sum(pick * label, 1, keepdims=True)
         live_key = jnp.sum(pick * live, 1, keepdims=True)
@@ -389,29 +437,40 @@
     ref[second, lanes] = value[32:]
 
 
+STREAMS = ((32, True), (32, True), (16, False), (16, False))
+
+
 def block_kernel(
-    tok_ref,
-    region_ref,
-    valid_ref,
-    wq_ref,
-    wp_ref,
+    scale_ref,
+    tok_hbm,
+    wq_hbm,
+    region_hbm,
+    valid_hbm,
+    table_hbm,
+    wp_hbm,
+    gain_attn_hbm,
     wm_hbm,
-    scale_ref,
-    table_ref,
-    gain_attn_ref,
-    gain_merge_ref,
-    cot_ref,
-    strip_ref,
-    quad_ref,
-    onehot_ref,
-    heads_ref,
+    gain_merge_hbm,
+    cot_hbm,
     merged_out,
     tokens_out,
     qkv_out,
     proj_out,
     merge_out,
     bias_out,
+    tok_ref,
+    wq_ref,
+    region_ref,
+    valid_ref,
+    table_ref,
+    wp_ref,
+    gain_attn_ref,
     wm_ref,
+    gain_merge_ref,
+    cot_ref,
+    strip_ref,
+    quad_ref,
+    onehot_ref,
     tw_ref,
     x_ref,
     qkv_ref,
@@ -448,23 +507,49 @@
     sum_d,
     *scratch,
 ):
-    many = len(stream_scratch(32))
-    bufs = [scratch[i * many : (i + 1) * many] for i in range(4)]
-    bias_bufs = scratch[4 * many : 4 * many + 4]
-    send, recv, local = scratch[4 * many + 4 :]
+    bufs, at = [], 0
+    for rows, ring in STREAMS:
+        many = len(stream_scratch(rows, ring))
+        bufs.append(scratch[at : at + many])
+        at += many
+    bias_bufs = scratch[at : at + 4]
+    send, recv, local = scratch[at + 4 :]
     place = Place()
     sems = Sems(send, recv)
-    load = pltpu.make_async_copy(wm_hbm, wm_ref, local)
-    load.start()
-
     strip = place.y * NZ + place.z
     image = place.x * CORES + place.c
     after = (lax.rem(strip + 1, NY * NZ), image)
     before = (lax.rem(strip + NY * NZ - 1, NY * NZ), image)
     own, far = slice(0, HALF), slice(HALF, TOKENS)
 
+    partners = place.partners() + [after, before]
+    greet(partners)
+    loads = {}
+    for index, (source, target) in enumerate(
+        (
+            (tok_hbm, tok_ref),
+            (wq_hbm, wq_ref),
+            (region_hbm, region_ref),
+            (valid_hbm, valid_ref),
+            (table_hbm, table_ref),
+            (wp_hbm, wp_ref),
+            (gain_attn_hbm, gain_attn_ref),
+            (wm_hbm, wm_ref),
+            (gain_merge_hbm, gain_merge_ref),
+            (cot_hbm, cot_ref),
+        )
+    ):
+        loads[id(target)] = pltpu.make_async_copy(source, target, local.at[index])
+        loads[id(target)].start()
+
+    def ready(*refs):
+        for ref in refs:
+            loads.pop(id(ref)).wait()
+
+    strip_ref[...] = strip_order()
+    ready(tok_ref)
     tw_ref[...] = nn(strip_ref[...], tok_ref[...]).astype(BF16)
-    enter(place.partners() + [after, before])
+    enter(partners)
     halo_tokens = sems.copy(tw_ref.at[own], x_ref.at[far], before)
     x_ref[own] = tw_ref[far]
 
@@ -477,14 +562,18 @@
         for h in range(4):
             row = row + masks[h] * scale_ref[g * 4 + h]
         scales.append(row)
-    heads = heads_ref[...]
-
+    ready(wq_ref)
     qkv_ref[own] = nn(x_ref[own], wq_ref[...]).astype(BF16)
+    ready(region_ref, valid_ref)
     window_masks(place, region_ref, valid_ref, mask_ref)
+    quad_ref[...] = quad_order()
+    onehot_ref[...] = offset_order()
+    ready(table_ref)
     spread_bias(table_ref, onehot_ref, padded_ref, grid_ref, bias_ref)
     halo_tokens.wait_recv()
     qkv_ref[far] = nn(x_ref[far], wq_ref[...]).astype(BF16)
 
+    heads = head_order()
     for g in range(GROUPS):
         cols = slice(g * LANES, (g + 1) * LANES)
         for part, high, low in ((0, qh_ref, ql_ref), (D, kh_ref, kl_ref)):
@@ -518,6 +607,7 @@
 
     lax.fori_loop(0, 4, forward, 0)
 
+    ready(wp_ref, gain_attn_ref)
     gain_attn = gain_attn_ref[...]
 
     def project(rows):
@@ -540,7 +630,7 @@
             ]
 
     make_quads(1, normed_ref[own])
-    load.wait()
+    ready(wm_ref, gain_merge_ref, cot_ref)
     halo_normed.wait_recv()
     make_quads(0, normed_in[...])
 
@@ -570,8 +660,8 @@
                 sum_b[c, y, x] = block[:, 1, :, lanes].reshape(NZ * 32, LANES).astype(BF16)
 
     tasks = [
-        stream(place, sems, "x", "y", 32, sum_a, merge_out.at[0:32], bufs[0]),
-        stream(place, sems, "y", "x", 32, sum_b, merge_out.at[32:64], bufs[1]),
+        stream(place, sems, "x", "y", 32, True, sum_a, merge_out.at[0:32], bufs[0]),
+        stream(place, sems, "y", "x", 32, True, sum_b, merge_out.at[32:64], bufs[1]),
     ]
 
     def pump():
@@ -593,9 +683,9 @@
         gm_ref[rows] = nt(go_ref[rows], wp_ref[...]).astype(BF16)
 
     back_norm(own, scale_own)
+    pump()
     halo_hidden.wait_recv()
     back_norm(far, scale_far)
-    pump()
 
     acc_ref[...] = jnp.zeros_like(acc_ref)
 
@@ -615,11 +705,8 @@
             put(dn_ref, w, start, fold_heads(tn(grad_score, take(kh_ref, w, start)), masks))
         return carry
 
-    lax.fori_loop(0, 2, backward, 0)
+    lax.fori_loop(0, 4, backward, 0)
     pump()
-    lax.fori_loop(2, 4, backward, 0)
-    pump()
-
     for g in range(GROUPS):
         for part in (0, D):
             cols = slice(part + g * LANES, part + (g + 1) * LANES)
@@ -649,8 +736,8 @@
                 sum_c[c, x, y] = one[rows]
                 sum_d[c, y, x] = two[rows]
     tasks += [
-        stream(place, sems, "x", "y", 16, sum_c, part_a, bufs[2]),
-        stream(place, sems, "y", "x", 16, sum_d, part_b, bufs[3]),
+        stream(place, sems, "x", "y", 16, False, sum_c, part_a, bufs[2]),
+        stream(place, sems, "y", "x", 16, False, sum_d, part_b, bufs[3]),
         bias_sum(place, sems, bias_part, padded_ref, bias_bufs),
     ]
     pump()
@@ -678,7 +765,9 @@
 def block(tokens, region, valid, wq, wp, wm, scale, table, gain_attn, gain_merge, cot):
     vmem = pl.BlockSpec(memory_space=pltpu.VMEM)
     smem = pl.BlockSpec(memory_space=pltpu.SMEM)
-    total = 4 + 4 * STREAM_COPIES + BIAS_COPIES
+    far = pl.BlockSpec(memory_space=pl.ANY)
+    total = 4 + sum(stream_copies(ring) for _, ring in STREAMS) + BIAS_COPIES
+    inputs = [tokens, wq, region, valid, table, wp, gain_attn, wm, gain_merge, cot]
 
     def buf(*shape):
         return pltpu.VMEM(shape, BF16)
@@ -696,10 +785,13 @@
             jax.ShapeDtypeStruct((64, 128), F32),
             jax.ShapeDtypeStruct((16, OFFSETS), F32),
         ],
-        in_specs=[vmem] * 5 + [pl.BlockSpec(memory_space=pl.ANY), smem] + [vmem] * 8,
+        in_specs=[smem] + [far] * len(inputs),
         out_specs=[vmem] * 6,
-        scratch_shapes=[
-            buf(2048, 1024),
+        scratch_shapes=[pltpu.VMEM(value.shape, value.dtype) for value in inputs]
+        + [
+            buf(TOKENS, TOKENS),
+            buf(HALF, HALF),
+            buf(256, 1024),
             buf(TOKENS, D),
             buf(TOKENS, D),
             buf(TOKENS, 3 * D),
@@ -735,21 +827,41 @@
             buf(CORES, NX, NY, NZ * 16, LANES),
             buf(CORES, NY, NX, NZ * 16, LANES),
         ]
-        + stream_scratch(32)
-        + stream_scratch(32)
-        + stream_scratch(16)
-        + stream_scratch(16)
+        + sum([stream_scratch(*kind) for kind in STREAMS], [])
         + bias_scratch()
         + [
             pltpu.SemaphoreType.DMA((total,)),
             pltpu.SemaphoreType.DMA((total,)),
-            pltpu.SemaphoreType.DMA,
+            pltpu.SemaphoreType.DMA((len(inputs),)),
         ],
         compiler_params=pltpu.CompilerParams(
             collective_id=0, has_side_effects=True, vmem_limit_bytes=56 * 1024 * 1024
         ),
         name="block",
-    )(tokens, region, valid, wq, wp, wm, scale, table, gain_attn, gain_merge, cot, *constants())
+    )(scale, *inputs)
+
+
+def hand_out_kernel(*refs):
+    count = len(refs) // 2
+    copies = [
+        pltpu.make_async_copy(refs[i], refs[count + i], refs[-1].at[i]) for i in range(count)
+    ]
+    for copy in copies:
+        copy.start()
+    for copy in copies:
+        copy.wait()
+
+
+def hand_out(values):
+    near, far = pl.BlockSpec(memory_space=pltpu.VMEM), pl.BlockSpec(memory_space=pl.ANY)
+    return pl.pallas_call(
+        hand_out_kernel,
+        out_shape=[jax.ShapeDtypeStruct(value.shape, value.dtype) for value in values],
+        in_specs=[near] * len(values),
+        out_specs=[far] * len(values),
+        scratch_shapes=[pltpu.SemaphoreType.DMA((len(values),))],
+        name="hand_out",
+    )(*values)
 
 
 def shards(
@@ -765,10 +877,11 @@
     gain_merge,
     cotangent,
 ):
-    merged, grad_tokens, grad_qkv, grad_proj, grad_merge, grad_bias = block(
+    merged, grad_tokens, grad_qkv, grad_proj, grad_merge, grad_bias = hand_out(
+        block(
         tokens.reshape(TOKENS, D),
-        region[0],
-        valid[0],
+        region[0].T,
+        valid[0].T,
         qkv_weight,
         proj_weight,
         merge_weight,
@@ -777,7 +890,7 @@
         gain_attn[None],
         gain_merge[None],
         cotangent.reshape(64, 1024),
-    )
+    ))
     return (
         merged.reshape(cotangent.shape),
         grad_tokens.reshape(tokens.shape),

time: 92.5 us -> 73.5 us (0.79)
  local copies, waits for them, and re-layouts: 11.4 us -> 0 us
  Pallas kernels: 79.4 us -> 72.2 us
    unnamed x8 -> x0, local copies, waits for them, and re-layouts: 11.4 us -> none
    pallas_call x1, Pallas kernels: 79.4 us -> 70.4 us  [block(): pl.pallas_call(block_kernel, out_shape=[jax.ShapeDtypeStruct((64, 1024),...]
    pallas_call x0 -> x1, Pallas kernels: none -> 1.82 us  [hand_out(): pl.pallas_call(hand_out_kernel, out_shape=[jax.ShapeDtypeStruct(value.sha...]
where the time goes in v1:
time: 73.5 us; the launch traced here: 72.8 us
  Pallas kernels  72.2 us (98%)
    pallas_call x1, Pallas kernels, block(): pl.pallas_call(block_kernel, out_shape=[jax.ShapeDtypeStruct((64, 1024),...  70.4 us
    pallas_call x1, Pallas kernels, hand_out(): pl.pallas_call(hand_out_kernel, out_shape=[jax.ShapeDtypeStruct(value.sha...  1.82 us

profile of v1, /device:TPU:32, one launch (start us, length us, event | category | flops | bytes accessed | tf_op | source)
XLA Modules:
  0.0 72.8 jit_solution(1139053096416948895)
XLA Ops:
  0.6 70.4 %block.1 = (bf16[64,1024]{1,0:T(8,128)(2,1)}, bf16[256,512]{1,0:T(8,128)(2,1)}, f32[16,192]{1,0:T(8,128)}, f32[16,64]{1,0:T(8,128)}, f32[64,128]{1,0:T(8,128)}, /*index=5*/f32[16,225]{1,0:T(8,128)}) custom-call(f32[16]{0:T(128)} %scale_ref.1, bf16[256,512]{1,0:T(8,128)(2,1)} %bitcast.12, bf16[512,1536]{1,0:T(8,128)(2,1)} %wq_hbm.1, s32[8,64]{1,0:T(8,128)} %bitcast.15, ...), custom_call_target="tpu_custom_call" | custom-call | tf_op jit(solution)/shard_map/block/pallas_call | solution.py:778
  71.0 1.8 %hand_out.1 = (bf16[64,1024]{1,0:T(8,128)(2,1)}, bf16[256,512]{1,0:T(8,128)(2,1)}, f32[16,192]{1,0:T(8,128)}, f32[16,64]{1,0:T(8,128)}, f32[64,128]{1,0:T(8,128)}, /*index=5*/f32[16,225]{1,0:T(8,128)}) custom-call(bf16[64,1024]{1,0:T(8,128)(2,1)} %get-tuple-element.18.refs_0_, bf16[256,512]{1,0:T(8,128)(2,1)} %get-tuple-element.19.refs_1_, ...), custom_call_target="tpu_custom_call" | custom-call | tf_op jit(solution)/shard_map/hand_out/pallas_call | solution.py:857

commit v2 on v1

--- a/solution.py
+++ b/solution.py
@@ -75,16 +75,20 @@
         lax.fori_loop(0, count, body, 0)
 
 
-def ring_sum(place, sems, axis, held, blocks, far_lo, far_hi, from_dn, from_up, put_out):
+def ring_sum(place, sems, axis, held, prepare, blocks, far_lo, far_hi, from_dn, from_up, put_out):
     me = getattr(place, axis)
     up, dn, far = lax.rem(me + 1, 4), lax.rem(me + 3, 4), lax.rem(me + 2, 4)
     to_up, to_dn = place.along(axis, 1), place.along(axis, 3)
     half = blocks // 2
     lo, hi = pl.ds(0, half), pl.ds(half, half)
+    prepare(far)
     one = sems.copy(held.at[far, lo], far_lo, to_up)
     two = sems.copy(held.at[far, hi], far_hi, to_dn)
+    prepare(up)
     three = sems.copy(held.at[up, hi], from_dn.at[hi], to_up)
+    prepare(dn)
     four = sems.copy(held.at[dn, lo], from_up.at[lo], to_dn)
+    prepare(me)
     yield
 
     def put_up(i, v):
@@ -96,7 +100,6 @@
     one.wait_recv()
     add_blocks(half, put_up, [lambda i: held[up, i], lambda i: far_lo[i]])
     five = sems.copy(held.at[up, lo], from_dn.at[lo], to_up)
-    yield
     two.wait_recv()
     add_blocks(half, put_dn, [lambda i: held[dn, half + i], lambda i: far_hi[i]])
     six = sems.copy(held.at[dn, hi], from_up.at[hi], to_dn)
@@ -112,14 +115,16 @@
         copy.wait_send()
 
 
-def shot_sum(place, sems, axis, count, held, parts, blocks, arrived, out):
+def shot_sum(place, sems, axis, count, held, prepare, parts, blocks, arrived, out):
     me = getattr(place, axis)
     sent = []
     for step in range(1, count):
         target = lax.rem(me + step, count)
+        prepare(target)
         sent.append(
             sems.copy(held.at[target], arrived.at[step - 1], place.along(axis, step))
         )
+    prepare(me)
     yield
     for copy in sent:
         copy.wait_recv()
@@ -151,18 +156,34 @@
 
 
 def stream_copies(ring):
-    return 1 + (6 if ring else 3) + 3 + (NZ - 1)
-
-
-def stream(place, sems, first, second, rows, ring, source, out, bufs):
-    other, core, one, late, two, last = bufs[:6]
-    mine = place.c
-    cross = sems.copy(source.at[1 - mine], other, place.along("c", 1))
-    yield
-    cross.wait_recv()
-
-    def put_core(i, v):
-        core[i // 4, lax.rem(i, 4)] = v
+    return NX + (6 if ring else 3) + 3 + (NZ - 1)
+
+
+class CorePart:
+    def __init__(self, place, sems, x_first, source, other):
+        self.place, self.sems, self.x_first = place, sems, x_first
+        self.source, self.other, self.sent = source, other, []
+
+    def send(self, x):
+        across, theirs = self.place.along("c", 1), 1 - self.place.c
+        if self.x_first:
+            pair = self.source.at[theirs, x], self.other.at[x]
+        else:
+            pair = self.source.at[theirs, :, x], self.other.at[:, x]
+        self.sent.append(self.sems.copy(*pair, across))
+
+
+def stream(place, sems, first, second, rows, ring, cores, out, bufs):
+    core, one, late, two, last = bufs[1:6]
+    source, other, mine = cores.source, cores.other, place.c
+    for copy in cores.sent:
+        copy.wait_recv()
+
+    def add_core(k):
+        def put_core(i, v):
+            core[k, i] = v
+
+        add_blocks(4, put_core, [lambda i: source[mine, k, i], lambda i: other[k, i]])
 
     def put_one(i, v):
         one[i] = v.reshape(NZ, rows, LANES)
@@ -170,22 +191,17 @@
     def put_two(i, v):
         two[...] = v
 
-    add_blocks(
-        16,
-        put_core,
-        [
-            lambda i: source[mine, i // 4, lax.rem(i, 4)],
-            lambda i: other[i // 4, lax.rem(i, 4)],
-        ],
-    )
+    def nothing(k):
+        pass
+
     if ring:
-        yield from ring_sum(place, sems, first, core, 4, *bufs[6:], put_one)
+        yield from ring_sum(place, sems, first, core, add_core, 4, *bufs[6:], put_one)
     else:
         yield from shot_sum(
-            place, sems, first, 4, core, lambda ref, k, i: ref[k, i], 4, bufs[6], put_one
+            place, sems, first, 4, core, add_core, lambda ref, k, i: ref[k, i], 4, bufs[6], put_one
         )
     yield from shot_sum(
-        place, sems, second, 4, one, lambda ref, k, i: ref[k], 1, late, put_two
+        place, sems, second, 4, one, nothing, lambda ref, k, i: ref[k], 1, late, put_two
     )
     sent = []
     for step in range(1, NZ):
@@ -197,9 +213,8 @@
         sent[step - 1].wait_recv()
         total = total + last[step - 1].astype(jnp.float32)
     out[...] = total
-    for copy in sent:
+    for copy in sent + cores.sent:
         copy.wait_send()
-    cross.wait_send()
 
 
 BIAS_ROWS, BIAS_LANES = 16, 256
@@ -233,14 +248,12 @@
         copy.wait_send()
 
 
-def run_all(tasks):
-    tasks = list(tasks)
-    while tasks:
-        for task in list(tasks):
-            try:
-                next(task)
-            except StopIteration:
-                tasks.remove(task)
+def advance(tasks):
+    for task in list(tasks):
+        try:
+            next(task)
+        except StopIteration:
+            tasks.remove(task)
 
 
 def greet(partners):
@@ -489,6 +502,9 @@
     hat_ref,
     normed_in,
     quads_ref,
+    xt_ref,
+    mixedt_ref,
+    quadst_ref,
     gh_ref,
     gn_ref,
     go_ref,
@@ -589,23 +605,28 @@
 
     def forward(w, carry):
         allowed = mask_ref[w] > 0.5
+        scores = []
         for g in range(GROUPS):
             start = g * LANES
             kh, kl = take(kh_ref, w, start), take(kl_ref, w, start)
             qh = stack_heads(take(qh_ref, w, start), masks16)
             ql = stack_heads(take(ql_ref, w, start), masks16)
-            score = nt(
-                jnp.concatenate([kh, kl, kh], axis=1), jnp.concatenate([qh, qh, ql], axis=1)
+            scores.append(
+                nt(jnp.concatenate([kh, kl, kh], axis=1), jnp.concatenate([qh, qh, ql], axis=1))
             )
-            score = jnp.where(allowed, score + bias_ref[g], -1000000000.0)
+        rounded = []
+        for g in range(GROUPS):
+            score = jnp.where(allowed, scores[g] + bias_ref[g], -1000000000.0)
             expo = jnp.exp(score - jnp.max(score, 0, keepdims=True))
             probs = expo * (1.0 / jnp.sum(expo, 0, keepdims=True))
             probs_ref[w, g] = probs
-            out = tn(probs.astype(BF16), take(qkv_ref, w, 2 * D + start))
-            put(mixed_ref, w, start, fold_heads(out, masks).astype(BF16))
+            rounded.append(probs.astype(BF16))
+        outs = [tn(rounded[g], take(qkv_ref, w, 2 * D + g * LANES)) for g in range(GROUPS)]
+        for g in range(GROUPS):
+            put(mixed_ref, w, g * LANES, fold_heads(outs[g], masks).astype(BF16))
         return carry
 
-    lax.fori_loop(0, 4, forward, 0)
+    lax.fori_loop(0, 4, forward, 0, unroll=2)
 
     ready(wp_ref, gain_attn_ref)
     gain_attn = gain_attn_ref[...]
@@ -630,14 +651,33 @@
             ]
 
     make_quads(1, normed_ref[own])
+    xt_ref[...] = x_ref[...].T
+    mixedt_ref[...] = mixed_ref[...].T
     ready(wm_ref, gain_merge_ref, cot_ref)
     halo_normed.wait_recv()
     make_quads(0, normed_in[...])
+    quadst_ref[...] = quads_ref[...].T
 
     gain_merge = gain_merge_ref[...]
     hat, scale = norm_parts(nn(quads_ref[...], wm_ref[...]))
     merged_out[...] = (hat * gain_merge).astype(BF16)
     grad_pre = norm_back(cot_ref[...].astype(F32) * gain_merge, hat, scale).astype(BF16)
+    parts_a = CorePart(place, sems, True, sum_a, bufs[0][0])
+    parts_b = CorePart(place, sems, False, sum_b, bufs[1][0])
+    parts_c = CorePart(place, sems, True, sum_c, bufs[2][0])
+    parts_d = CorePart(place, sems, False, sum_d, bufs[3][0])
+    for x in range(NX):
+        for y in range(NY):
+            block = nn(
+                quadst_ref[y * D : (y + 1) * D], grad_pre[:, x * 256 : (x + 1) * 256]
+            ).reshape(NZ, 2, 32, 256)
+            for c in range(CORES):
+                lanes = slice(c * LANES, (c + 1) * LANES)
+                sum_a[c, x, y] = block[:, 0, :, lanes].reshape(NZ * 32, LANES).astype(BF16)
+                sum_b[c, y, x] = block[:, 1, :, lanes].reshape(NZ * 32, LANES).astype(BF16)
+        parts_a.send(x)
+        parts_b.send(x)
+
     grad_quads = nt(grad_pre, wm_ref[...]).astype(BF16)
     for which in range(2):
         stacked = jnp.concatenate(
@@ -649,29 +689,14 @@
             halo_hidden = sems.copy(gh_ref.at[own], gn_ref.at[far], before)
     gn_ref[own] = gh_ref[far]
 
-    for x in range(NX):
-        for y in range(NY):
-            block = tn(
-                quads_ref[:, y * D : (y + 1) * D], grad_pre[:, x * 256 : (x + 1) * 256]
-            ).reshape(NZ, 2, 32, 256)
-            for c in range(CORES):
-                lanes = slice(c * LANES, (c + 1) * LANES)
-                sum_a[c, x, y] = block[:, 0, :, lanes].reshape(NZ * 32, LANES).astype(BF16)
-                sum_b[c, y, x] = block[:, 1, :, lanes].reshape(NZ * 32, LANES).astype(BF16)
-
-    tasks = [
-        stream(place, sems, "x", "y", 32, True, sum_a, merge_out.at[0:32], bufs[0]),
-        stream(place, sems, "y", "x", 32, True, sum_b, merge_out.at[32:64], bufs[1]),
+    merging = [
+        stream(place, sems, "x", "y", 32, True, parts_a, merge_out.at[0:32], bufs[0]),
+        stream(place, sems, "y", "x", 32, True, parts_b, merge_out.at[32:64], bufs[1]),
     ]
-
-    def pump():
-        for task in list(tasks):
-            try:
-                next(task)
-            except StopIteration:
-                tasks.remove(task)
-
-    pump()
+    attending = [
+        stream(place, sems, "x", "y", 16, False, parts_c, part_a, bufs[2]),
+        stream(place, sems, "y", "x", 16, False, parts_d, part_b, bufs[3]),
+    ]
 
     def back_norm(rows, scale):
         grad = gn_ref[rows].astype(F32) * gain_attn
@@ -683,30 +708,37 @@
         gm_ref[rows] = nt(go_ref[rows], wp_ref[...]).astype(BF16)
 
     back_norm(own, scale_own)
-    pump()
+    advance(merging)
     halo_hidden.wait_recv()
     back_norm(far, scale_far)
 
     acc_ref[...] = jnp.zeros_like(acc_ref)
 
     def backward(w, carry):
+        starts = [g * LANES for g in range(GROUPS)]
+        grads = [stack_heads(take(gm_ref, w, start), masks16) for start in starts]
+        grad_probs = [
+            nt(take(qkv_ref, w, 2 * D + start), grad) for start, grad in zip(starts, grads)
+        ]
+        for g, start in enumerate(starts):
+            value = nn(probs_ref[w, g].astype(BF16), grads[g])
+            put(act_ref, w, 2 * D + start, value.astype(BF16))
+        grad_scores = []
         for g in range(GROUPS):
-            start = g * LANES
-            grad = stack_heads(take(gm_ref, w, start), masks16)
             probs = probs_ref[w, g]
-            grad_probs = nt(take(qkv_ref, w, 2 * D + start), grad)
-            put(act_ref, w, 2 * D + start, nn(probs.astype(BF16), grad).astype(BF16))
-            weighted = probs * grad_probs
+            weighted = probs * grad_probs[g]
             grad_score = weighted - probs * jnp.sum(weighted, 0, keepdims=True)
             acc_ref[g] += grad_score
-            grad_score = grad_score.astype(BF16)
+            grad_scores.append(grad_score.astype(BF16))
+        for g, start in enumerate(starts):
             query = stack_heads(take(qh_ref, w, start), masks16)
-            put(dn_ref, w, D + start, nn(grad_score, query))
-            put(dn_ref, w, start, fold_heads(tn(grad_score, take(kh_ref, w, start)), masks))
+            put(dn_ref, w, D + start, nn(grad_scores[g], query))
+        outs = [tn(grad_scores[g], take(kh_ref, w, starts[g])) for g in range(GROUPS)]
+        for g, start in enumerate(starts):
+            put(dn_ref, w, start, fold_heads(outs[g], masks))
         return carry
 
-    lax.fori_loop(0, 4, backward, 0)
-    pump()
+    lax.fori_loop(0, 4, backward, 0, unroll=2)
     for g in range(GROUPS):
         for part in (0, D):
             cols = slice(part + g * LANES, part + (g + 1) * LANES)
@@ -717,15 +749,12 @@
             unit = qkv_ref[:, cols].astype(F32) * inverse
             act_ref[:, cols] = (inverse * (grad - unit * head_sum(unit * grad, heads))).astype(BF16)
 
-    gs_ref[far] = nt(act_ref[far], wq_ref[...]).astype(BF16)
-    halo_shifted = sems.copy(gs_ref.at[far], gs_in, after)
-    pump()
-
-    bias_part = gather_bias(acc_ref, onehot_ref, grid_ref)
+    advance(merging)
+
     left = iota((1, LANES), 1) < 64
     for x in range(NX):
-        block = tn(x_ref[...], act_ref[:, x * 384 : (x + 1) * 384])
-        rolled = tn(mixed_ref[...], roll_ref[:, x * LANES : (x + 1) * LANES])
+        block = nn(xt_ref[...], act_ref[:, x * 384 : (x + 1) * 384])
+        rolled = nn(mixedt_ref[...], roll_ref[:, x * LANES : (x + 1) * LANES])
         middle = block[:, 128:256]
         firsts = (block[:, :128], block[:, 256:])
         seconds = (jnp.where(left, middle, rolled), jnp.where(left, rolled, middle))
@@ -735,21 +764,28 @@
                 rows = slice(y * 128, (y + 1) * 128)
                 sum_c[c, x, y] = one[rows]
                 sum_d[c, y, x] = two[rows]
-    tasks += [
-        stream(place, sems, "x", "y", 16, False, sum_c, part_a, bufs[2]),
-        stream(place, sems, "y", "x", 16, False, sum_d, part_b, bufs[3]),
-        bias_sum(place, sems, bias_part, padded_ref, bias_bufs),
-    ]
-    pump()
-
+        parts_c.send(x)
+        parts_d.send(x)
+
+    gs_ref[far] = nt(act_ref[far], wq_ref[...]).astype(BF16)
+    halo_shifted = sems.copy(gs_ref.at[far], gs_in, after)
+    advance(attending)
+
+    bias_part = gather_bias(acc_ref, onehot_ref, grid_ref)
+    biasing = [bias_sum(place, sems, bias_part, padded_ref, bias_bufs)]
+    advance(biasing)
     gs_ref[own] = nt(act_ref[own], wq_ref[...]).astype(BF16)
     gs_ref[own] = (gh_ref[far].astype(F32) + gs_ref[own].astype(F32)).astype(BF16)
+    advance(biasing)
     halo_shifted.wait_recv()
     gn_own = (gh_ref[own].astype(F32) + gs_in[...].astype(F32)).astype(BF16)
     tokens_out[...] = tn(strip_ref[...], jnp.concatenate([gn_own, gs_ref[own]], axis=0)).astype(
         BF16
     )
-    run_all(tasks)
+    while merging or attending or biasing:
+        advance(attending)
+        advance(merging)
+        advance(biasing)
     for copy in (halo_tokens, halo_normed, halo_hidden, halo_shifted):
         copy.wait_send()
 
@@ -810,6 +846,9 @@
             wide(TOKENS, D),
             buf(HALF, D),
             buf(64, 2048),
+            buf(D, TOKENS),
+            buf(D, TOKENS),
+            buf(2048, 64),
             buf(TOKENS, D),
             buf(TOKENS, D),
             buf(TOKENS, D),

time: 73.5 us -> 67.1 us (0.913)
  Pallas kernels: 72.2 us -> 65.4 us
    pallas_call x1, Pallas kernels: 70.4 us -> 63.6 us  [block(): pl.pallas_call(block_kernel, out_shape=[jax.ShapeDtypeStruct((64, 1024),...]
where the time goes in v2:
time: 67.1 us; the launch traced here: 66.2 us
  Pallas kernels  65.4 us (97%)
  between operations  0.8 us (1%)
    pallas_call x1, Pallas kernels, block(): pl.pallas_call(block_kernel, out_shape=[jax.ShapeDtypeStruct((64, 1024),...  63.6 us
    pallas_call x1, Pallas kernels, hand_out(): pl.pallas_call(hand_out_kernel, out_shape=[jax.ShapeDtypeStruct(value.sha...  1.82 us

profile of v2, /device:TPU:32, one launch (start us, length us, event | category | flops | bytes accessed | tf_op | source)
XLA Modules:
  0.0 66.2 jit_solution(4170384503827830471)
XLA Ops:
  0.6 63.6 %block.1 = (bf16[64,1024]{1,0:T(8,128)(2,1)}, bf16[256,512]{1,0:T(8,128)(2,1)}, f32[16,192]{1,0:T(8,128)}, f32[16,64]{1,0:T(8,128)}, f32[64,128]{1,0:T(8,128)}, /*index=5*/f32[16,225]{1,0:T(8,128)}) custom-call(f32[16]{0:T(128)} %scale_ref.1, bf16[256,512]{1,0:T(8,128)(2,1)} %bitcast.12, bf16[512,1536]{1,0:T(8,128)(2,1)} %wq_hbm.1, s32[8,64]{1,0:T(8,128)} %bitcast.15, ...), custom_call_target="tpu_custom_call" | custom-call | tf_op jit(solution)/shard_map/block/pallas_call | solution.py:814
  64.2 1.8 %hand_out.1 = (bf16[64,1024]{1,0:T(8,128)(2,1)}, bf16[256,512]{1,0:T(8,128)(2,1)}, f32[16,192]{1,0:T(8,128)}, f32[16,64]{1,0:T(8,128)}, f32[64,128]{1,0:T(8,128)}, /*index=5*/f32[16,225]{1,0:T(8,128)}) custom-call(bf16[64,1024]{1,0:T(8,128)(2,1)} %get-tuple-element.18.refs_0_, bf16[256,512]{1,0:T(8,128)(2,1)} %get-tuple-element.19.refs_1_, ...), custom_call_target="tpu_custom_call" | custom-call | tf_op jit(solution)/shard_map/hand_out/pallas_call | solution.py:896

commit v3 on v2

--- a/solution.py
+++ b/solution.py
@@ -566,7 +566,10 @@
     ready(tok_ref)
     tw_ref[...] = nn(strip_ref[...], tok_ref[...]).astype(BF16)
     enter(partners)
-    halo_tokens = sems.copy(tw_ref.at[own], x_ref.at[far], before)
+    halo_tokens = [
+        sems.copy(tw_ref.at[pl.ds(at, 64)], x_ref.at[pl.ds(HALF + at, 64)], before)
+        for at in (0, 64)
+    ]
     x_ref[own] = tw_ref[far]
 
     lane = iota((1, LANES), 1)
@@ -579,30 +582,30 @@
             row = row + masks[h] * scale_ref[g * 4 + h]
         scales.append(row)
     ready(wq_ref)
+    heads = head_order()
+
+    def normalise(rows):
+        for part, high, low in ((0, qh_ref, ql_ref), (D, kh_ref, kl_ref)):
+            columns = [slice(part + g * LANES, part + (g + 1) * LANES) for g in range(GROUPS)]
+            raws = [qkv_ref[rows, cols].astype(F32) for cols in columns]
+            sums = [head_sum(raw * raw, heads) for raw in raws]
+            for g, cols in enumerate(columns):
+                inverse = lax.rsqrt(sums[g] + 1e-06)
+                inv_ref[rows, cols] = inverse
+                unit = raws[g] * inverse
+                if part == 0:
+                    unit = unit * scales[g]
+                near = slice(g * LANES, (g + 1) * LANES)
+                high[rows, near], low[rows, near] = split2(unit)
+
     qkv_ref[own] = nn(x_ref[own], wq_ref[...]).astype(BF16)
+    normalise(own)
     ready(region_ref, valid_ref)
     window_masks(place, region_ref, valid_ref, mask_ref)
     quad_ref[...] = quad_order()
     onehot_ref[...] = offset_order()
     ready(table_ref)
     spread_bias(table_ref, onehot_ref, padded_ref, grid_ref, bias_ref)
-    halo_tokens.wait_recv()
-    qkv_ref[far] = nn(x_ref[far], wq_ref[...]).astype(BF16)
-
-    heads = head_order()
-    for g in range(GROUPS):
-        cols = slice(g * LANES, (g + 1) * LANES)
-        for part, high, low in ((0, qh_ref, ql_ref), (D, kh_ref, kl_ref)):
-            raw = qkv_ref[:, part + g * LANES : part + (g + 1) * LANES].astype(F32)
-            inverse = lax.rsqrt(head_sum(raw * raw, heads) + 1e-06)
-            inv_ref[:, part + g * LANES : part + (g + 1) * LANES] = inverse
-            unit = raw * inverse
-            if part == 0:
-                unit = unit * scales[g]
-            a, b = split2(unit)
-            high[:, cols] = a
-            low[:, cols] = b
-
     def forward(w, carry):
         allowed = mask_ref[w] > 0.5
         scores = []
@@ -626,8 +629,6 @@
             put(mixed_ref, w, g * LANES, fold_heads(outs[g], masks).astype(BF16))
         return carry
 
-    lax.fori_loop(0, 4, forward, 0, unroll=2)
-
     ready(wp_ref, gain_attn_ref)
     gain_attn = gain_attn_ref[...]
 
@@ -637,8 +638,19 @@
         normed_ref[rows] = (hat * gain_attn).astype(BF16)
         return scale
 
-    scale_far = project(far)
-    halo_normed = sems.copy(normed_ref.at[far], normed_in, after)
+    pieces = [(at, slice(HALF + at, HALF + at + 64)) for at in (0, 64)]
+    halo_normed, scales_far = [], []
+    for index, (at, rows) in enumerate(pieces):
+        halo_tokens[index].wait_recv()
+        qkv_ref[rows] = nn(x_ref[rows], wq_ref[...]).astype(BF16)
+        normalise(rows)
+        lax.fori_loop(2 * index, 2 * index + 2, forward, 0, unroll=2)
+        scales_far.append(project(rows))
+        halo_normed.append(
+            sems.copy(
+                normed_ref.at[pl.ds(HALF + at, 64)], normed_in.at[pl.ds(at, 64)], after
+            )
+        )
     scale_own = project(own)
 
     def make_quads(which, added):
@@ -654,7 +666,8 @@
     xt_ref[...] = x_ref[...].T
     mixedt_ref[...] = mixed_ref[...].T
     ready(wm_ref, gain_merge_ref, cot_ref)
-    halo_normed.wait_recv()
+    for copy in halo_normed:
+        copy.wait_recv()
     make_quads(0, normed_in[...])
     quadst_ref[...] = quads_ref[...].T
 
@@ -686,7 +699,10 @@
         )
         gh_ref[which * HALF : (which + 1) * HALF] = tn(quad_ref[...], stacked).astype(BF16)
         if which == 0:
-            halo_hidden = sems.copy(gh_ref.at[own], gn_ref.at[far], before)
+            halo_hidden = [
+                sems.copy(gh_ref.at[pl.ds(at, 64)], gn_ref.at[pl.ds(HALF + at, 64)], before)
+                for at in (0, 64)
+            ]
     gn_ref[own] = gh_ref[far]
 
     merging = [
@@ -709,9 +725,6 @@
 
     back_norm(own, scale_own)
     advance(merging)
-    halo_hidden.wait_recv()
-    back_norm(far, scale_far)
-
     acc_ref[...] = jnp.zeros_like(acc_ref)
 
     def backward(w, carry):
@@ -738,18 +751,19 @@
             put(dn_ref, w, start, fold_heads(outs[g], masks))
         return carry
 
-    lax.fori_loop(0, 4, backward, 0, unroll=2)
-    for g in range(GROUPS):
-        for part in (0, D):
-            cols = slice(part + g * LANES, part + (g + 1) * LANES)
-            grad = dn_ref[:, cols]
-            if part == 0:
-                grad = grad * scales[g]
-            inverse = inv_ref[:, cols]
-            unit = qkv_ref[:, cols].astype(F32) * inverse
-            act_ref[:, cols] = (inverse * (grad - unit * head_sum(unit * grad, heads))).astype(BF16)
-
-    advance(merging)
+    for index, (at, rows) in enumerate(pieces):
+        halo_hidden[index].wait_recv()
+        back_norm(rows, scales_far[index])
+        lax.fori_loop(2 * index, 2 * index + 2, backward, 0, unroll=2)
+    for part in (0, D):
+        columns = [slice(part + g * LANES, part + (g + 1) * LANES) for g in range(GROUPS)]
+        grads = [dn_ref[:, cols] for cols in columns]
+        if part == 0:
+            grads = [grad * scale for grad, scale in zip(grads, scales)]
+        units = [qkv_ref[:, cols].astype(F32) * inv_ref[:, cols] for cols in columns]
+        sums = [head_sum(unit * grad, heads) for unit, grad in zip(units, grads)]
+        for g, cols in enumerate(columns):
+            act_ref[:, cols] = (inv_ref[:, cols] * (grads[g] - units[g] * sums[g])).astype(BF16)
 
     left = iota((1, LANES), 1) < 64
     for x in range(NX):
@@ -767,6 +781,7 @@
         parts_c.send(x)
         parts_d.send(x)
 
+    advance(merging)
     gs_ref[far] = nt(act_ref[far], wq_ref[...]).astype(BF16)
     halo_shifted = sems.copy(gs_ref.at[far], gs_in, after)
     advance(attending)
@@ -783,10 +798,10 @@
         BF16
     )
     while merging or attending or biasing:
+        advance(merging)
         advance(attending)
-        advance(merging)
         advance(biasing)
-    for copy in (halo_tokens, halo_normed, halo_hidden, halo_shifted):
+    for copy in halo_tokens + halo_normed + halo_hidden + [halo_shifted]:
         copy.wait_send()
 
     bias_out[...] = padded_ref[:, :OFFSETS]
@@ -802,7 +817,7 @@
     vmem = pl.BlockSpec(memory_space=pltpu.VMEM)
     smem = pl.BlockSpec(memory_space=pltpu.SMEM)
     far = pl.BlockSpec(memory_space=pl.ANY)
-    total = 4 + sum(stream_copies(ring) for _, ring in STREAMS) + BIAS_COPIES
+    total = 7 + sum(stream_copies(ring) for _, ring in STREAMS) + BIAS_COPIES
     inputs = [tokens, wq, region, valid, table, wp, gain_attn, wm, gain_merge, cot]
 
     def buf(*shape):

time: 67.1 us -> 62.4 us (0.930); the launches traced: 66.2 us -> 62.2 us
  Pallas kernels: 65.4 us -> 61.4 us
    pallas_call x1, Pallas kernels: 63.6 us -> 59.6 us  [block(): pl.pallas_call(block_kernel, out_shape=[jax.ShapeDtypeStruct((64, 1024),...]
where the time goes in v3:
time: 62.4 us; the launch traced here: 62.2 us
  Pallas kernels  61.4 us (98%)
  between operations  0.8 us (1%)
    pallas_call x1, Pallas kernels, block(): pl.pallas_call(block_kernel, out_shape=[jax.ShapeDtypeStruct((64, 1024),...  59.6 us
    pallas_call x1, Pallas kernels, hand_out(): pl.pallas_call(hand_out_kernel, out_shape=[jax.ShapeDtypeStruct(value.sha...  1.82 us

profile of v3, /device:TPU:32, one launch (start us, length us, event | category | flops | bytes accessed | tf_op | source)
XLA Modules:
  0.0 62.2 jit_solution(16750527541489237303)
XLA Ops:
  0.6 59.6 %block.1 = (bf16[64,1024]{1,0:T(8,128)(2,1)}, bf16[256,512]{1,0:T(8,128)(2,1)}, f32[16,192]{1,0:T(8,128)}, f32[16,64]{1,0:T(8,128)}, f32[64,128]{1,0:T(8,128)}, /*index=5*/f32[16,225]{1,0:T(8,128)}) custom-call(f32[16]{0:T(128)} %scale_ref.1, bf16[256,512]{1,0:T(8,128)(2,1)} %bitcast.12, bf16[512,1536]{1,0:T(8,128)(2,1)} %wq_hbm.1, s32[8,64]{1,0:T(8,128)} %bitcast.15, ...), custom_call_target="tpu_custom_call" | custom-call | tf_op jit(solution)/shard_map/block/pallas_call | solution.py:829
  60.3 1.8 %hand_out.1 = (bf16[64,1024]{1,0:T(8,128)(2,1)}, bf16[256,512]{1,0:T(8,128)(2,1)}, f32[16,192]{1,0:T(8,128)}, f32[16,64]{1,0:T(8,128)}, f32[64,128]{1,0:T(8,128)}, /*index=5*/f32[16,225]{1,0:T(8,128)}) custom-call(bf16[64,1024]{1,0:T(8,128)(2,1)} %get-tuple-element.18.refs_0_, bf16[256,512]{1,0:T(8,128)(2,1)} %get-tuple-element.19.refs_1_, ...), custom_call_target="tpu_custom_call" | custom-call | tf_op jit(solution)/shard_map/hand_out/pallas_call | solution.py:911

commit v4 on v3

--- a/solution.py
+++ b/solution.py
@@ -465,12 +465,14 @@
     wm_hbm,
     gain_merge_hbm,
     cot_hbm,
-    merged_out,
-    tokens_out,
+    merged_hbm,
+    tokens_hbm,
     qkv_out,
     proj_out,
     merge_out,
     bias_out,
+    merged_out,
+    tokens_out,
     tok_ref,
     wq_ref,
     region_ref,
@@ -674,6 +676,8 @@
     gain_merge = gain_merge_ref[...]
     hat, scale = norm_parts(nn(quads_ref[...], wm_ref[...]))
     merged_out[...] = (hat * gain_merge).astype(BF16)
+    write_merged = pltpu.make_async_copy(merged_out, merged_hbm, local.at[10])
+    write_merged.start()
     grad_pre = norm_back(cot_ref[...].astype(F32) * gain_merge, hat, scale).astype(BF16)
     parts_a = CorePart(place, sems, True, sum_a, bufs[0][0])
     parts_b = CorePart(place, sems, False, sum_b, bufs[1][0])
@@ -797,6 +801,8 @@
     tokens_out[...] = tn(strip_ref[...], jnp.concatenate([gn_own, gs_ref[own]], axis=0)).astype(
         BF16
     )
+    write_tokens = pltpu.make_async_copy(tokens_out, tokens_hbm, local.at[11])
+    write_tokens.start()
     while merging or attending or biasing:
         advance(merging)
         advance(attending)
@@ -805,6 +811,8 @@
         copy.wait_send()
 
     bias_out[...] = padded_ref[:, :OFFSETS]
+    write_merged.wait()
+    write_tokens.wait()
     one, two = part_a[...], part_b[...]
     one_rolled, two_rolled = pltpu.roll(one, 64, 1), pltpu.roll(two, 64, 1)
     first_core = place.c == 0
@@ -837,8 +845,9 @@
             jax.ShapeDtypeStruct((16, OFFSETS), F32),
         ],
         in_specs=[smem] + [far] * len(inputs),
-        out_specs=[vmem] * 6,
-        scratch_shapes=[pltpu.VMEM(value.shape, value.dtype) for value in inputs]
+        out_specs=[far] * 2 + [vmem] * 4,
+        scratch_shapes=[buf(64, 1024), buf(TOKENS, D)]
+        + [pltpu.VMEM(value.shape, value.dtype) for value in inputs]
         + [
             buf(TOKENS, TOKENS),
             buf(HALF, HALF),
@@ -886,7 +895,7 @@
         + [
             pltpu.SemaphoreType.DMA((total,)),
             pltpu.SemaphoreType.DMA((total,)),
-            pltpu.SemaphoreType.DMA((len(inputs),)),
+            pltpu.SemaphoreType.DMA((len(inputs) + 2,)),
         ],
         compiler_params=pltpu.CompilerParams(
             collective_id=0, has_side_effects=True, vmem_limit_bytes=56 * 1024 * 1024

time: 62.4 us -> 62.3 us (level)
  no operation moved by 1% of the time
where the time goes in v4:
time: 62.3 us; the launch traced here: 62.2 us
  Pallas kernels  61.4 us (99%)
  between operations  0.8 us (1%)
    pallas_call x1, Pallas kernels, block(): pl.pallas_call(block_kernel, out_shape=[jax.ShapeDtypeStruct((64, 1024),...  59.6 us
    pallas_call x1, Pallas kernels, hand_out(): pl.pallas_call(hand_out_kernel, out_shape=[jax.ShapeDtypeStruct(value.sha...  1.82 us

profile of v4, /device:TPU:32, one launch (start us, length us, event | category | flops | bytes accessed | tf_op | source)
XLA Modules:
  0.0 62.2 jit_solution(6203159838197771105)
XLA Ops:
  0.6 59.6 %block.1 = (bf16[64,1024]{1,0:T(8,128)(2,1)}, bf16[256,512]{1,0:T(8,128)(2,1)}, f32[16,192]{1,0:T(8,128)}, f32[16,64]{1,0:T(8,128)}, f32[64,128]{1,0:T(8,128)}, /*index=5*/f32[16,225]{1,0:T(8,128)}) custom-call(f32[16]{0:T(128)} %scale_ref.1, bf16[256,512]{1,0:T(8,128)(2,1)} %bitcast.12, bf16[512,1536]{1,0:T(8,128)(2,1)} %wq_hbm.1, s32[8,64]{1,0:T(8,128)} %bitcast.15, ...), custom_call_target="tpu_custom_call" | custom-call | tf_op jit(solution)/shard_map/block/pallas_call | solution.py:837
  60.2 1.8 %hand_out.1 = (bf16[64,1024]{1,0:T(8,128)(2,1)}, bf16[256,512]{1,0:T(8,128)(2,1)}, f32[16,192]{1,0:T(8,128)}, f32[16,64]{1,0:T(8,128)}, f32[64,128]{1,0:T(8,128)}, /*index=5*/f32[16,225]{1,0:T(8,128)}) custom-call(bf16[64,1024]{1,0:T(8,128)(2,1)} %get-tuple-element.18.refs_0_, bf16[256,512]{1,0:T(8,128)(2,1)} %get-tuple-element.19.refs_1_, ...), custom_call_target="tpu_custom_call" | custom-call | tf_op jit(solution)/shard_map/hand_out/pallas_call | solution.py:920
